TPU v7x, 256 devices: a whole 4x4x8 slice. The times are simulated.
256 devices in a mesh: rel: 8 (over z_lo, core), ent: 32 (over x, z_hi, y).
Axes of the slice: x: 4, y: 4, z: 8 (z_hi: 2, z_lo: 4; z = z_hi * 4 + z_lo), core: 2. Of those that a mesh axis runs over, the one named last changes fastest.
Arguments:
- facts: bfloat16 [64, 4096, 4096], P('rel', 'ent'), may hold values from -6 to 6
- observed: int32 [64, 4096, 316], P('rel', 'ent'), may hold values from 0 to 8191
- factors: bfloat16 [4096, 128], P('ent'), may hold values from -0.59765625 to 0.59765625
- cores: bfloat16 [64, 128, 128], P('rel'), may hold values from -6 to 6
Outputs:
- grad_factors: float32 [4096, 128], P('ent')
- grad_cores: float32 [64, 128, 128], P('rel')
All inputs are finite; a program needn't handle non-finite values.
Results may differ from a plain program's by a relative error of at most 0.0008.
Values may be sent and summed in bfloat16 or wider, within the bound.
A program may use at most 128 MiB of HBM per device.

v0:
```python
import jax
import jax.numpy as jnp
from jax import lax
from jax.sharding import PartitionSpec as P


def unpack(words, count):
    shifts = jnp.arange(13, dtype=jnp.int32)
    bits = jnp.bitwise_and(jnp.right_shift(words[..., None], shifts), 1)
    flat = bits.reshape(words.shape[:-1] + (words.shape[-1] * 13,))
    return flat[..., :count].astype(jnp.bfloat16)


def per_device(facts, observed, factors, cores):
    n_all = facts.shape[2]
    rel_loc, ent_loc, rank = (cores.shape[0], factors.shape[0], factors.shape[1])
    n_rel = rel_loc * lax.axis_size("rel")
    mask = unpack(observed, n_all)
    left = jnp.einsum("ir,krs->kis", factors, cores, preferred_element_type=jnp.float32).astype(
        jnp.bfloat16
    )
    piece = lax.all_gather(factors, "ent", axis=0, tiled=True)
    right = jnp.einsum("js,krs->kjr", piece, cores, preferred_element_type=jnp.float32).astype(
        jnp.bfloat16
    )
    model = jnp.einsum("kis,js->kij", left, piece, preferred_element_type=jnp.float32)
    data = facts.astype(jnp.float32)
    marks = mask.astype(jnp.float32)
    err = (marks * (model - data)).astype(jnp.bfloat16)
    own_rows = jnp.einsum("kij,kjr->ir", err, right, preferred_element_type=jnp.float32)
    block = jnp.einsum("kij,kis->js", err, left, preferred_element_type=jnp.float32)
    all_rows = block
    pull_sum = jnp.einsum("kij,js->kis", err, piece, preferred_element_type=jnp.float32)
    own_rows, all_rows, pull_sum = (own_rows, all_rows, pull_sum)
    offset = lax.axis_index("ent") * ent_loc
    mine = lax.dynamic_slice_in_dim(all_rows, offset, ent_loc, 0)
    partial_value = lax.dynamic_update_slice_in_dim(all_rows, mine + own_rows, offset, 0)
    shared = lax.psum_scatter(partial_value, "ent", scatter_dimension=0, tiled=True)
    owned = lax.psum(shared, "rel")
    grad_factors = owned / jnp.sqrt(jnp.float32(n_all * n_rel))
    pull = pull_sum.astype(jnp.bfloat16)
    core_part = jnp.einsum("ir,kis->krs", factors, pull, preferred_element_type=jnp.float32)
    core_grad = lax.psum(core_part, "ent")
    grad_cores = core_grad * (rank / n_all)
    return (grad_factors, grad_cores)


def solution(mesh):
    return jax.shard_map(
        per_device,
        mesh=mesh,
        in_specs=(
            P("rel", "ent", None),
            P("rel", "ent", None),
            P("ent", None),
            P("rel", None, None),
        ),
        out_specs=(P("ent", None), P("rel", None, None)),
        check_vma=False,
    )
```

profile of v0, /device:TPU:1, one launch (start us, length us, event | category | flops | bytes accessed | tf_op | source)
XLA Modules:
  0.0 907.8 jit_solution(7252655520066823902)
XLA Ops:
  7.2 0.0 copy-start
  7.2 0.0 all-gather.2.cloned.1.call-start
  7.2 0.7 all-gather.2.cloned.1.call-update
  7.9 0.0 reduce-scatter.2.cloned.1.call-start
  8.0 12.1 %copy.20 = bf16[8,128,4096]{1,0,2:T(8,128)(2,1)} copy(bf16[8,128,4096]{2,1,0:T(8,128)(2,1)} %param.4) | data formatting | bytes 16777216 | tf_op args[0]
  20.1 0.2 shift_right_arithmetic.23
  20.3 0.0 copy-start.7
  20.3 0.3 fusion.2
  20.6 0.0 copy-start.4
  20.6 74.8 %all-gather.2.cloned.1.call-done = bf16[4096,128]{1,0:T(8,128)(2,1)} async-done(((bf16[128,128]{1,0:T(8,128)(2,1)}), bf16[4096,128]{1,0:T(8,128)(2,1)}) %all-gather.2.cloned.1.call-update) | async-done | bytes 1048592 | tf_op jit(solution)/shard_map/all_gather | solution.py:22
  95.4 9.3 %fusion.8 = f32[8,128,4096]{2,1,0:T(8,128)} fusion(bf16[8,128,128]{1,2,0:T(8,128)(2,1)S(1)} %fusion.2, bf16[4096,128]{1,0:T(8,128)(2,1)} %all-gather.2.cloned.1.call-done), kind=kOutput, calls=%fused_computation.15 | convolution fusion | flops 1073741824 | bytes 18087936 | tf_op jit(solution)/shard_map/kis,js->kij/dot_general | solution.py:26
  104.8 17.6 %copy.21 = f32[8,128,4096]{1,0,2:T(8,128)} copy(f32[8,128,4096]{2,1,0:T(8,128)} %fusion.8) | data formatting | bytes 33554432 | tf_op jit(solution)/shard_map/kis,js->kij/dot_general | solution.py:26
  122.4 1.1 shift_right_arithmetic.20
  123.5 15.2 %multiply_convert_fusion = bf16[8,128,4096]{1,0,2:T(8,128)(2,1)} fusion(f32[8,128,4096]{1,0,2:T(8,128)} %copy.21, bf16[8,128,4096]{1,0,2:T(8,128)(2,1)} %copy.20, s32[8,128,4108]{1,0,2:T(8,128)S(1)} %bitcast.36, s32[4096]{0:T(1024)S(1)} %slice-done), kind=kLoop, calls=%fused_computation.3 | loop fusion | flops 33554432 | bytes 50348032 | tf_op jit(solution)/shard_map/convert_element_type | solution.py:29
  138.6 11.9 %copy.26 = bf16[8,128,4096]{2,1,0:T(8,128)(2,1)} copy(bf16[8,128,4096]{1,0,2:T(8,128)(2,1)} %multiply_convert_fusion) | data formatting | bytes 16777216 | tf_op jit(solution)/shard_map/convert_element_type | solution.py:29
  150.5 5.8 convolution_bitcast_fusion
  156.4 5.6 convert_bitcast_fusion
  162.0 12.0 %copy.33 = bf16[8,4096,128]{2,0,1:T(8,128)(2,1)} copy(bf16[8,4096,128]{1,2,0:T(8,128)(2,1)} %convert_bitcast_fusion) | data formatting | bytes 16777216 | tf_op jit(solution)/shard_map/convert_element_type | solution.py:23
  173.9 8.3 fusion.4
  182.3 1.4 copy-done.2
  183.6 0.0 reduce-scatter.2.cloned.1.call-update
  183.7 0.0 all-reduce.5.cloned.1.call-start
  183.7 6.7 convolution_bitcast_fusion.1
  190.5 0.0 all-reduce.5.cloned.1.call-update
  190.5 0.0 all-reduce.3.cloned.1.call-start
  190.5 193.7 %reduce-scatter.2.cloned.1.call-done = f32[128,128]{1,0:T(8,128)} async-done(((f32[4096,128]{1,0:T(8,128)}), f32[128,128]{1,0:T(8,128)}) %reduce-scatter.2.cloned.1.call-update) | async-done | bytes 65552 | tf_op jit(solution)/shard_map/reduce_scatter | solution.py:38
  384.2 0.0 all-reduce.3.cloned.1.call-update
  384.2 425.5 %all-reduce.5.cloned.1.call-done = f32[8,128,128]{1,2,0:T(8,128)} async-done(((f32[8,128,128]{1,2,0:T(8,128)}), f32[8,128,128]{1,2,0:T(8,128)}) %all-reduce.5.cloned.1.call-update) | async-done | bytes 524304 | tf_op jit(solution)/shard_map/psum | solution.py:43
  809.7 1.1 broadcast_multiply_fusion
  810.8 1.0 copy.28
  811.8 88.1 %all-reduce.3.cloned.1.call-done = f32[128,128]{1,0:T(8,128)} async-done(((f32[128,128]{1,0:T(8,128)}), f32[128,128]{1,0:T(8,128)}) %all-reduce.3.cloned.1.call-update) | async-done | bytes 65552 | tf_op jit(solution)/shard_map/psum | solution.py:39
  899.8 1.5 broadcast_multiply_fusion.1
  (15 shorter events, 0.0 us)
Async XLA Ops:
  7.2 13.2 %copy-start = (bf16[8,128,128]{2,1,0:T(8,128)(2,1)S(1)}, bf16[8,128,128]{2,1,0:T(8,128)(2,1)}, u32[]{:S(2)}) copy-start(bf16[8,128,128]{2,1,0:T(8,128)(2,1)} %param.7) | copy-start | bytes 786436
  7.2 88.3 %all-gather.2.cloned.1.call-start = ((), (), s32[]{:S(2)}) async-start(), calls=%async_computation.1 | async-start | bytes 1081344 | tf_op jit(solution)/shard_map/all_gather | solution.py:22
  7.9 376.3 %reduce-scatter.2.cloned.1.call-start = ((), (), s32[]{:S(2)}) async-start(), calls=%async_computation.2 | async-start | bytes 2162688 | tf_op jit(solution)/shard_map/reduce_scatter | solution.py:38
  8.0 12.4 %copy-start.6 = (bf16[128,128]{1,0:T(8,128)(2,1)S(1)}, bf16[128,128]{1,0:T(8,128)(2,1)}, u32[]{:S(2)}) copy-start(bf16[128,128]{1,0:T(8,128)(2,1)} %param.6) | copy-start | bytes 98308
  20.3 84.5 %copy-start.7 = (s32[4108]{0:T(1024)}, s32[4108]{0:T(1024)S(1)}, u32[]{:S(2)}) copy-start(s32[4108]{0:T(1024)S(1)} %shift_right_arithmetic.23) | copy-start | bytes 49300
  20.6 84.2 %copy-start.4 = (bf16[8,128,128]{1,2,0:T(8,128)(2,1)}, bf16[8,128,128]{1,2,0:T(8,128)(2,1)S(1)}, u32[]{:S(2)}) copy-start(bf16[8,128,128]{1,2,0:T(8,128)(2,1)S(1)} %fusion.2) | copy-start | bytes 786436
  104.8 17.6 %copy-start.5 = (s32[8,128,316]{1,0,2:T(8,128)S(1)}, s32[8,128,316]{1,0,2:T(8,128)}, u32[]{:S(2)}) copy-start(s32[8,128,316]{1,0,2:T(8,128)} %param.5) | copy-start | bytes 3883012
  122.4 1.1 slice-start
  150.5 5.9 copy-start.3
  173.9 727.4 %copy-start.1 = (bf16[8,128,128]{2,1,0:T(8,128)(2,1)S(1)}, bf16[8,128,128]{2,1,0:T(8,128)(2,1)}, u32[]{:S(2)}) copy-start(bf16[8,128,128]{2,1,0:T(8,128)(2,1)} %param.7) | copy-start | bytes 786436
  182.3 1.4 copy-start.2
  183.7 626.0 %all-reduce.5.cloned.1.call-start = ((), (), s32[]{:S(2)}) async-start(), calls=%async_computation.4 | async-start | bytes 1048576 | tf_op jit(solution)/shard_map/psum | solution.py:43
  190.5 709.3 %all-reduce.3.cloned.1.call-start = ((), (), s32[]{:S(2)}) async-start(), calls=%async_computation.3 | async-start | bytes 131072 | tf_op jit(solution)/shard_map/psum | solution.py:39
Sparse Core Ops, SparseCore 0:
  11.4 83.9 all-gather.1
  183.8 200.3 reduce-scatter.1
  387.6 422.0 all-reduce.4
  812.1 87.6 all-reduce.2
where the time goes:
time: 911 us; the launch traced here: 908 us
  waiting for transfers between devices  783 us (86%)
  local copies, waits for them, and re-layouts  57.2 us (6%)
  matrix products  36.1 us (4%)
  other arithmetic  17.7 us (2%)
  between operations  13.9 us (2%)
    psum x1, waiting for transfers between devices, per_device(): core_grad = lax.psum(core_part, 'ent')  425 us
    reduce_scatter x1, waiting for transfers between devices, per_device(): lax.psum_scatter(partial_value, 'ent', scatter_dimension=0, tiled=True)  194 us
    psum x1, waiting for transfers between devices, per_device(): owned = lax.psum(shared, 'rel')  88.1 us
    all_gather x1, waiting for transfers between devices, per_device(): piece = lax.all_gather(factors, 'ent', axis=0, tiled=True)  74.8 us
  transfers between devices with their start and end apart: 4, of which 4 were waited for; matrix products, arithmetic and copies ran while one was open for 2% of the time, Pallas kernels for 0%

commit v1 on v0

v1 whole, which is shorter than its diff:
```python
import math

import jax
import jax.numpy as jnp
from jax import lax
from jax.experimental import pallas as pl
from jax.experimental.pallas import tpu as pltpu
from jax.sharding import PartitionSpec as P

F32, BF16 = jnp.float32, jnp.bfloat16
MESH = pl.DeviceIdType.MESH
NT = (((1,), (1,)), ((), ()))
WIDE = BF16

COUNTS = dict(
    a1=3, z=2, a2=3, b1=3, b2=3, fwd=8, swap=8, r1=6, r2=6, zr=8, own=1, fin=1,
    k1=6, k2=6, k3=1, k4=6, k5=6,
)
BASE, TOTAL = {}, 0
for _name, _count in COUNTS.items():
    BASE[_name] = TOTAL
    TOTAL += _count


def unpack(obs_ref, mask_ref, k):
    words = obs_ref[k]
    n_words = words.shape[1]
    n_tiles = mask_ref.shape[2] // 128
    both = jnp.bitwise_or(words[0:64], jnp.left_shift(words[64:128], 16))
    sources = []
    for first in range(0, n_words, 128):
        part = both[:, first : first + 128]
        if part.shape[1] < 128:
            fill = jnp.zeros((64, 128 - part.shape[1]), jnp.int32)
            part = jnp.concatenate([part, fill], axis=1)
        sources.append(part)
    lane = lax.broadcasted_iota(jnp.int32, (64, 128), 1)
    for q in range(13):
        column = lane + 128 * q
        word = (column * 5042) >> 16
        low = jnp.left_shift(1, column - word * 13)
        high = jnp.left_shift(low, 16)
        for period, source in enumerate(sources):
            tile = 13 * period + q
            if tile >= n_tiles:
                continue
            spread = jnp.take_along_axis(source, word, axis=1, mode="promise_in_bounds")
            at = slice(128 * tile, 128 * tile + 128)
            mask_ref[k, 0:64, at] = jnp.where((spread & low) != 0, 1.0, 0.0).astype(BF16)
            mask_ref[k, 64:128, at] = jnp.where((spread & high) != 0, 1.0, 0.0).astype(BF16)


def kernel(
    facts_hbm, obs_hbm, fac_hbm, cores_hbm, gf_ref, gc_ref,
    facts, obs, fac, cores, mask, left, left_t, err, pull, pull_hi, spread_f,
    blk, swapped, acc, r1_out, r1_in, r2_in, ring, own, own_in, total, total_in,
    part, k1_in, k_sum, k2_in, k_small, k3_in, k_final,
    local, send, recv,
):
    rel, ent = lax.axis_index("rel"), lax.axis_index("ent")
    zl, h = rel // 2, rel % 2
    x, zh, y = ent // 8, (ent // 4) % 2, ent % 4
    z = zh * 4 + zl
    other = 1 - h

    def dev(x=x, y=y, zh=zh, zl=zl, c=h):
        return {"rel": zl * 2 + c, "ent": x * 8 + zh * 4 + y}

    xp = lambda d: (x + d + 4) % 4
    yp = lambda d: (y + d + 4) % 4
    sibling = dev(c=other)

    def message(kind, index, src, dst, to):
        at = BASE[kind] + index
        return pltpu.make_async_remote_copy(
            src_ref=src, dst_ref=dst, send_sem=send.at[at], recv_sem=recv.at[at],
            device_id=to, device_id_type=MESH,
        )

    def start(kind, index, src, dst, to):
        message(kind, index, src, dst, to).start()

    def arrive(kind, index, dst):
        message(kind, index, dst, dst, sibling).wait_recv()

    def sent(kind, index, src):
        message(kind, index, src, src, sibling).wait_send()

    loads = [
        pltpu.make_async_copy(fac_hbm, fac, local.at[0]),
        pltpu.make_async_copy(obs_hbm, obs, local.at[1]),
        pltpu.make_async_copy(cores_hbm, cores, local.at[2]),
        pltpu.make_async_copy(facts_hbm, facts, local.at[3]),
    ]
    for load in loads:
        load.start()
    barrier = pltpu.get_barrier_semaphore()
    greeted = (
        [dev(x=xp(d)) for d in (1, 2, 3)]
        + [dev(y=yp(d)) for d in (1, 2, 3)]
        + [dev(zh=(z + d) % 8 // 4, zl=(z + d) % 4) for d in range(1, 8)]
        + [sibling]
    )
    for device in greeted:
        pl.semaphore_signal(barrier, inc=1, device_id=device, device_id_type=MESH)

    loads[1].wait()

    def one_mask(k, carry):
        unpack(obs, mask, k)
        return carry

    lax.fori_loop(0, obs.shape[0], one_mask, 0)
    pull[...] = jnp.zeros_like(pull)
    loads[0].wait()
    half = pl.ds(pl.multiple_of(h * 64, 64), 64)
    other_half = pl.ds(pl.multiple_of(other * 64, 64), 64)
    spread_f[0, y, x, h] = fac[half, :]

    pl.semaphore_wait(barrier, len(greeted))

    for d in (1, 2, 3):
        start("a1", d - 1, fac.at[half, :], spread_f.at[0, y, x, h], dev(x=xp(d)))
    near = ((0, 3, 2), (3, 0, 1))
    for source, *targets in near:
        @pl.when(zl == source)
        def _():
            for i, target in enumerate(targets):
                start(
                    "z", i, fac.at[half, :], spread_f.at[1, x, y, h], dev(zh=1 - zh, zl=target)
                )

    loads[2].wait()
    for k in range(cores.shape[0]):
        rows = slice(128 * k, 128 * k + 128)
        value = jnp.dot(fac[...], cores[k], preferred_element_type=F32)
        left[rows, :] = value.astype(BF16)
        left_t[:, rows] = value.T.astype(BF16)

    for d in (1, 2, 3):
        arrive("a1", d - 1, spread_f.at[0, y, xp(-d), h])
    row = spread_f.at[0, y, :, h]
    for d in (1, 2, 3):
        start("a2", d - 1, row, row, dev(y=yp(d)))
    start("fwd", 0, row, row, sibling)
    for source, *targets in near:
        for i, target in enumerate(targets):
            @pl.when(zl == target)
            def _():
                arrive("z", i, spread_f.at[1, x, y, h])
    for d in (1, 2, 3):
        start("b1", d - 1, spread_f.at[1, x, y, h], spread_f.at[1, x, y, h], dev(y=yp(d)))
    loads[3].wait()

    column = spread_f.at[1, x, :, h]

    def place(t):
        third = (t + 1) // 3
        later = (third + 1) // 2
        part_of = (t % 2) * (1 - later) + third // 2
        d = later * ((t + 1) % 3 + 1)
        group = (y + part_of * (x - y) - d + 4) % 4
        return part_of, group

    def settle(t):
        part_of, group = place(t)
        arrive("swap", t, swapped.at[t])

        @pl.when(t < 2)
        def _():
            acc[part_of] = blk[t, half, :] + swapped[t]

        @pl.when(t >= 2)
        def _():
            r1_out[t - 2] = (blk[t, half, :] + swapped[t]).astype(r1_out.dtype)

        @pl.when((t >= 2) & (t < 5))
        def _():
            start("r1", t - 2, r1_out.at[t - 2], r1_in.at[t - 2], dev(y=group))

        @pl.when(t >= 5)
        def _():
            start("r1", t - 2, r1_out.at[t - 2], r1_in.at[t - 2], dev(x=group))

    def step(t, carry):
        part_of, group = place(t)

        @pl.when(t == 1)
        def _():
            for d in (1, 2, 3):
                arrive("b1", d - 1, spread_f.at[1, x, yp(-d), h])
            for d in (1, 2, 3):
                start("b2", d - 1, column, column, dev(x=xp(d)))
            start("fwd", 1, column, column, sibling)

        @pl.when(t == 2)
        def _():
            for d in (1, 2, 3):
                block = spread_f.at[0, yp(-d), :, h]
                arrive("a2", d - 1, block)
                start("fwd", 1 + d, block, block, sibling)

        @pl.when(t == 5)
        def _():
            for d in (1, 2, 3):
                block = spread_f.at[1, xp(-d), :, h]
                arrive("b2", d - 1, block)
                start("fwd", 4 + d, block, block, sibling)

        arrive("fwd", t, spread_f.at[part_of, group, :, other])
        rows = spread_f[part_of, group].reshape(512, 128)
        model = lax.dot_general(left[...], rows, NT, preferred_element_type=F32)
        for m in range(4):
            entity = (1 - part_of) * (m * 8 + zh * 4 + group) + part_of * (
                group * 8 + (1 - zh) * 4 + m
            )
            at = pl.ds(pl.multiple_of(entity * 128, 128), 128)
            for k in range(cores.shape[0]):
                here = slice(128 * k, 128 * k + 128)
                there = slice(128 * m, 128 * m + 128)
                diff = model[here, there] - facts[k, :, at].astype(F32)
                err[here, there] = diff.astype(BF16) * mask[k, :, at]
        pull[...] += jnp.dot(err[...], rows, preferred_element_type=F32)
        blk[t] = jnp.dot(left_t[...], err[...], preferred_element_type=F32)
        start("swap", t, blk.at[t, other_half, :], swapped.at[t], sibling)

        @pl.when(t >= 1)
        def _():
            settle(t - 1)

        return carry

    lax.fori_loop(0, 8, step, 0)

    fac_t = fac[...].astype(F32).T.astype(BF16)
    pull_hi[...] = pull[...].astype(BF16)
    for k in range(cores.shape[0]):
        rows = slice(128 * k, 128 * k + 128)
        part[k] = jnp.dot(fac_t, pull_hi[rows, :], preferred_element_type=F32)
    for d in (1, 2, 3):
        start("k1", d - 1, part.at[xp(d)], k1_in.at[d - 1], dev(x=xp(d)))
        start("k1", d + 2, part.at[4 + yp(d)], k1_in.at[d + 2], dev(y=yp(d)))
    own_value = jnp.zeros((128, 128), F32)
    for k in range(cores.shape[0]):
        rows = slice(128 * k, 128 * k + 128)
        high = pull_hi[rows, :]
        low = (pull[rows, :] - high.astype(F32)).astype(BF16)
        own_value += lax.dot_general(cores[k], high, NT, preferred_element_type=F32)
        own_value += lax.dot_general(cores[k], low, NT, preferred_element_type=F32)
    own[...] = own_value
    start("own", 0, own.at[other_half, :], own_in, sibling)
    settle(7)

    for d in range(6):
        arrive("k1", d, k1_in.at[d])
    k_sum[0] = part[x] + k1_in[0] + k1_in[1] + k1_in[2]
    k_sum[1] = part[4 + y] + k1_in[3] + k1_in[4] + k1_in[5]
    quarter = lambda i: pl.ds(pl.multiple_of(i * 32, 32), 32)
    for d in (1, 2, 3):
        start("k2", d - 1, k_sum.at[0, quarter(yp(d)), :], k2_in.at[d - 1], dev(y=yp(d)))
        start("k2", d + 2, k_sum.at[1, quarter(xp(d)), :], k2_in.at[d + 2], dev(x=xp(d)))

    for i in range(6):
        arrive("r1", i, r1_in.at[i])
    acc[0] = acc[0] + r1_in[0].astype(F32) + r1_in[1].astype(F32) + r1_in[2].astype(F32)
    acc[1] = acc[1] + r1_in[3].astype(F32) + r1_in[4].astype(F32) + r1_in[5].astype(F32)
    lanes = lambda i: pl.ds(pl.multiple_of(i * 128, 128), 128)
    for d in (1, 2, 3):
        start("r2", d - 1, acc.at[0, :, lanes(xp(d))], r2_in.at[d - 1], dev(x=xp(d)))
        start("r2", d + 2, acc.at[1, :, lanes(yp(d))], r2_in.at[d + 2], dev(y=yp(d)))

    for i in range(6):
        arrive("k2", i, k2_in.at[i])
    k_small[0, 0:32] = k_sum[0, quarter(y), :] + k2_in[0] + k2_in[1] + k2_in[2]
    k_small[0, 32:64] = k_sum[1, quarter(x), :] + k2_in[3] + k2_in[4] + k2_in[5]
    start("k3", 0, k_small.at[0], k3_in, dev(zh=1 - zh))

    arrive("own", 0, own_in)
    for i in range(6):
        arrive("r2", i, r2_in.at[i])
    ring[z] = (
        acc[0, :, lanes(x)] + r2_in[0] + r2_in[1] + r2_in[2] + own[half, :] + own_in[...]
    )
    total[0] = acc[1, :, lanes(y)] + r2_in[3] + r2_in[4] + r2_in[5]
    for d in (1, 2, 3):
        start("zr", d - 1, ring.at[z], ring.at[z], dev(zl=(zl + d) % 4))
    for d in range(4):
        start("zr", d + 3, total.at[0], ring.at[z], dev(zh=1 - zh, zl=(zl + d) % 4))

    n_all = facts.shape[2]
    n_rel = cores.shape[0] * lax.axis_size("rel")
    arrive("k3", 0, k3_in)
    k_small[1] = (k_small[0] + k3_in[...]) * (fac.shape[1] / n_all)
    mine = (
        pl.ds(pl.multiple_of(x * 128 + y * 32, 32), 32),
        pl.ds(pl.multiple_of(512 + y * 128 + x * 32, 32), 32),
    )
    k_final[mine[0], :] = k_small[1, 0:32]
    k_final[mine[1], :] = k_small[1, 32:64]
    for d in (1, 2, 3):
        start("k4", d - 1, k_small.at[1, 0:32, :], k_final.at[mine[0], :], dev(y=yp(d)))
        start("k4", d + 2, k_small.at[1, 32:64, :], k_final.at[mine[1], :], dev(x=xp(d)))
    for d in (1, 2, 3):
        at = pl.ds(pl.multiple_of(x * 128 + yp(-d) * 32, 32), 32)
        arrive("k4", d - 1, k_final.at[at, :])
        at = pl.ds(pl.multiple_of(512 + y * 128 + xp(-d) * 32, 32), 32)
        arrive("k4", d + 2, k_final.at[at, :])
    whole = lambda i: k_final.at[pl.ds(pl.multiple_of(i * 128, 128), 128), :]
    for d in (1, 2, 3):
        start("k5", d - 1, whole(x), whole(x), dev(x=xp(d)))
        start("k5", d + 2, whole(4 + y), whole(4 + y), dev(y=yp(d)))

    for d in (1, 2, 3):
        arrive("zr", d - 1, ring.at[zh * 4 + (zl - d + 4) % 4])
    for d in range(4):
        arrive("zr", d + 3, ring.at[(1 - zh) * 4 + (zl - d + 4) % 4])
    summed = ring[0]
    for i in range(1, 8):
        summed = summed + ring[i]
    total[1] = summed * (1.0 / math.sqrt(n_all * n_rel))
    start("fin", 0, total.at[1], total_in.at[h], sibling)
    total_in[h] = total[1]
    arrive("fin", 0, total_in.at[other])
    gf_ref[...] = total_in[...].reshape(gf_ref.shape).T

    for d in (1, 2, 3):
        arrive("k5", d - 1, whole(xp(-d)))
        arrive("k5", d + 2, whole(4 + yp(-d)))
    gc_ref[...] = k_final[...].reshape(gc_ref.shape)

    small = spread_f.at[0, 0, 0, 0]
    for d in range(3):
        sent("a1", d, small)
        sent("b1", d, small)
        sent("a2", d, column)
        sent("b2", d, column)
    for source, *targets in near:
        for i in range(len(targets)):
            @pl.when(zl == source)
            def _():
                sent("z", i, small)
    for t in range(8):
        sent("fwd", t, column)
        sent("swap", t, swapped.at[t])
    for i in range(6):
        sent("r1", i, r1_out.at[i])
        sent("r2", i, r2_in.at[i])
        sent("k1", i, k1_in.at[i])
        sent("k2", i, k2_in.at[i])
        sent("k4", i, k2_in.at[i])
        sent("k5", i, k1_in.at[i])
    for i in range(7):
        sent("zr", i, own_in)
    sent("own", 0, own_in)
    sent("fin", 0, own_in)
    sent("k3", 0, k3_in)


def per_device(facts, observed, factors, cores):
    n_rel, n_own, n_all = facts.shape
    rank = factors.shape[1]
    vmem = pltpu.VMEM
    anywhere = pl.BlockSpec(memory_space=pl.ANY)
    inside = pl.BlockSpec(memory_space=pltpu.VMEM)
    return pl.pallas_call(
        kernel,
        out_shape=(
            jax.ShapeDtypeStruct((n_own, rank), F32),
            jax.ShapeDtypeStruct((n_rel, rank, rank), F32),
        ),
        in_specs=[anywhere] * 4,
        out_specs=(inside, inside),
        scratch_shapes=[
            vmem(facts.shape, BF16),
            vmem(observed.shape, jnp.int32),
            vmem(factors.shape, BF16),
            vmem(cores.shape, BF16),
            vmem(facts.shape, BF16),
            vmem((n_rel * n_own, rank), BF16),
            vmem((rank, n_rel * n_own), BF16),
            vmem((n_rel * n_own, 512), BF16),
            vmem((n_rel * n_own, rank), F32),
            vmem((n_rel * n_own, rank), BF16),
            vmem((2, 4, 4, 2, 64, rank), BF16),
            vmem((8, rank, 512), F32),
            vmem((8, 64, 512), F32),
            vmem((2, 64, 512), F32),
            vmem((6, 64, 512), WIDE),
            vmem((6, 64, 512), WIDE),
            vmem((6, 64, 128), F32),
            vmem((8, 64, 128), F32),
            vmem((rank, n_own), F32),
            vmem((64, 128), F32),
            vmem((2, 64, 128), F32),
            vmem((2, 64, 128), F32),
            vmem((n_rel, rank, rank), F32),
            vmem((6, rank, rank), F32),
            vmem((2, rank, rank), F32),
            vmem((6, 32, rank), F32),
            vmem((2, 64, rank), F32),
            vmem((64, rank), F32),
            vmem((n_rel * rank, rank), F32),
            pltpu.SemaphoreType.DMA((4,)),
            pltpu.SemaphoreType.DMA((TOTAL,)),
            pltpu.SemaphoreType.DMA((TOTAL,)),
        ],
        compiler_params=pltpu.CompilerParams(
            collective_id=0, has_side_effects=True, vmem_limit_bytes=56 * 2**20
        ),
        cost_estimate=pl.CostEstimate(
            flops=6 * n_rel * n_own * n_all * rank,
            bytes_accessed=facts.size * 2 + observed.size * 4,
            transcendentals=0,
        ),
        name="rescal_gradients",
    )(facts, observed, factors, cores)


def solution(mesh):
    return jax.shard_map(
        per_device,
        mesh=mesh,
        in_specs=(
            P("rel", "ent", None),
            P("rel", "ent", None),
            P("ent", None),
            P("rel", None, None),
        ),
        out_specs=(P("ent", None), P("rel", None, None)),
        check_vma=False,
    )
```

time: 911 us -> 67.5 us (0.07)
  waiting for transfers between devices: 783 us -> 0 us
  Pallas kernels: 0 us -> 59.6 us
  local copies, waits for them, and re-layouts: 57.2 us -> 6.29 us
  matrix products: 36.1 us -> 0 us
  other arithmetic: 17.7 us -> 0 us
  between operations: 13.9 us -> 0.64 us
    psum x2 -> x0, waiting for transfers between devices: 514 us -> none  [the longest x1 425 us: per_device(): core_grad = lax.psum(core_part, 'ent')]
    reduce_scatter x1 -> x0, waiting for transfers between devices: 194 us -> none  [per_device(): lax.psum_scatter(partial_value, 'ent', scatter_dimension=0, tiled=True)]
    all_gather x1 -> x0, waiting for transfers between devices: 74.8 us -> none  [per_device(): piece = lax.all_gather(factors, 'ent', axis=0, tiled=True)]
    pallas_call x0 -> x1, Pallas kernels: none -> 59.6 us  [per_device(): pl.pallas_call(kernel, out_shape=(jax.ShapeDtypeStruct((n_own, rank), F32...]
    dot_general x6 -> x0, matrix products: 36.1 us -> none  [the longest x1 9.34 us: per_device(): jnp.einsum('kis,js->kij', left, piece, preferred_element_type=jnp.float32)]
    convert_element_type x2 -> x0, local copies, waits for them, and re-layouts: 23.9 us -> none  [the longest x1 12 us: per_device(): jnp.einsum('js,krs->kjr', piece, cores, preferred_element_type=jnp.float32)]
    dot_general x1 -> x0, local copies, waits for them, and re-layouts: 17.6 us -> none  [per_device(): jnp.einsum('kis,js->kij', left, piece, preferred_element_type=jnp.float32)]
    convert_element_type x1 -> x0, other arithmetic: 15.2 us -> none  [per_device(): err = (marks * (model - data)).astype(jnp.bfloat16)]
  transfers between devices with their start and end apart: 4 -> 0, of which waited for: 4 -> 0; matrix products, arithmetic and copies ran while one was open for 2% -> 0% of each run, Pallas kernels for 0% -> 0%
where the time goes in v1:
time: 67.5 us; the launch traced here: 66.5 us
  Pallas kernels  59.6 us (88%)
  local copies, waits for them, and re-layouts  6.29 us (9%)
    pallas_call x1, Pallas kernels, per_device(): pl.pallas_call(kernel, out_shape=(jax.ShapeDtypeStruct((n_own, rank), F32...  59.6 us
    unnamed x3, local copies, waits for them, and re-layouts  6.29 us

profile of v1, /device:TPU:1, one launch (start us, length us, event | category | flops | bytes accessed | tf_op | source)
XLA Modules:
  0.0 66.5 jit_solution(5453687210184932572)
XLA Ops:
  0.6 2.9 %copy.6.obs_hbm = s32[8,128,316]{2,1,0:T(8,128)} copy(s32[8,128,316]{1,0,2:T(8,128)} %param.5) | data formatting | bytes 2588672 | tf_op args[1]
  3.6 59.6 %rescal_gradients.1 = (f32[128,128]{1,0:T(8,128)}, f32[8,128,128]{2,1,0:T(8,128)}) custom-call(bf16[8,128,4096]{2,1,0:T(8,128)(2,1)} %facts_hbm.1, s32[8,128,316]{2,1,0:T(8,128)} %copy.6.obs_hbm, bf16[128,128]{1,0:T(8,128)(2,1)} %fac_hbm.1, bf16[8,128,128]{2,1,0:T(8,128)(2,1)} %cores_hbm.1), custom_call_target="tpu_custom_call" | custom-call | flops 3221225472 | bytes 9682944 | tf_op jit(solution)/shard_map/rescal_gradients/pallas_call | solution.py:365
  63.1 1.5 %copy.9 = f32[128,128]{1,0:T(8,128)} copy(f32[128,128]{1,0:T(8,128)} %get-tuple-element.4) | data formatting | bytes 131072
  64.6 1.9 %copy.10 = f32[8,128,128]{2,1,0:T(8,128)} copy(f32[8,128,128]{2,1,0:T(8,128)} %get-tuple-element.5) | data formatting | bytes 1048576

commit v2 on v0

v2 whole, which is shorter than its diff:
```python
import math

import jax
import jax.numpy as jnp
from jax import lax
from jax.experimental import pallas as pl
from jax.experimental.pallas import tpu as pltpu
from jax.sharding import PartitionSpec as P

F32, BF16 = jnp.float32, jnp.bfloat16
MESH = pl.DeviceIdType.MESH
NT = (((1,), (1,)), ((), ()))
ROWS_TYPE = BF16
CORE_TYPE = F32

COUNTS = dict(a=15, b=15, z=2, fwd=8, swap=8, r1=30, zr=7, own=1, fin=1, k1=15, k3=1, k5=15)
BASE, TOTAL = {}, 0
for _name, _count in COUNTS.items():
    BASE[_name] = TOTAL
    TOTAL += _count

PLANE = sorted(
    ((dx, dy) for dx in range(4) for dy in range(4) if dx or dy),
    key=lambda d: -(min(d[0], 4 - d[0]) + min(d[1], 4 - d[1])),
)
SLOT = lambda dx, dy: dx * 4 + dy - 1
ORDER = (0, 1, 3, 2)
NEAR = ((0, 3, 2), (3, 0, 1))


def unpack(obs, mask, k, n_words):
    rows = obs.shape[0] // 8
    low_half = obs[pl.ds(k, rows, stride=8), :]
    high_half = obs[pl.ds(k + 4, rows, stride=8), :]
    both = jnp.bitwise_or(low_half, jnp.left_shift(high_half, 16))
    sources = [both[first : first + 128].T for first in range(0, rows, 128)]
    n_tiles = mask.shape[2] // 128
    lane = lax.broadcasted_iota(jnp.int32, (128, 128), 1)
    for q in range(13):
        column = lane + 128 * q
        word = (column * 5042) >> 16
        low = jnp.left_shift(1, column - word * 13)
        high = jnp.left_shift(low, 16)
        for period, source in enumerate(sources):
            tile = 13 * period + q
            if tile >= n_tiles:
                continue
            spread = jnp.take_along_axis(source, word, axis=1, mode="promise_in_bounds")
            at = slice(128 * tile, 128 * tile + 128)
            mask[k, :, at] = jnp.where((spread & low) != 0, 1.0, 0.0).astype(BF16)
            mask[k + 4, :, at] = jnp.where((spread & high) != 0, 1.0, 0.0).astype(BF16)


def kernel(
    facts_hbm, obs_hbm, fac_hbm, cores_hbm, gf_ref, gc_hbm,
    facts, obs, fac, cores, mask, left, left_t, err, pull, pull_hi, spread_f,
    blk, swapped, acc, r1_out, r1_in, ring, own, own_in, total, total_in,
    part, k1_out, k1_in, k_small, k3_in, k_final,
    local, send, recv,
):
    rel, ent = lax.axis_index("rel"), lax.axis_index("ent")
    zl, h = rel // 2, rel % 2
    x, zh, y = ent // 8, (ent // 4) % 2, ent % 4
    z = zh * 4 + zl
    other = 1 - h
    n_words = obs_hbm.shape[0] // 8

    def dev(x=x, y=y, zh=zh, zl=zl, c=h):
        return {"rel": zl * 2 + c, "ent": x * 8 + zh * 4 + y}

    near_x = lambda d: (x + d + 4) % 4
    near_y = lambda d: (y + d + 4) % 4
    sibling = dev(c=other)
    pending = []

    def message(kind, index, src, dst, to):
        at = BASE[kind] + index
        return pltpu.make_async_remote_copy(
            src_ref=src, dst_ref=dst, send_sem=send.at[at], recv_sem=recv.at[at],
            device_id=to, device_id_type=MESH,
        )

    def start(kind, index, src, dst, to, track=True):
        message(kind, index, src, dst, to).start()
        if track:
            pending.append((kind, index, src))

    def arrive(kind, index, dst):
        message(kind, index, dst, dst, sibling).wait_recv()

    def sent(kind, index, src):
        message(kind, index, src, src, sibling).wait_send()

    loads = [
        pltpu.make_async_copy(obs_hbm, obs.at[pl.ds(0, n_words * 8), :], local.at[1]),
        pltpu.make_async_copy(fac_hbm, fac, local.at[0]),
        pltpu.make_async_copy(cores_hbm, cores, local.at[2]),
        pltpu.make_async_copy(facts_hbm, facts, local.at[3]),
    ]
    for load in loads:
        load.start()
    barrier = pltpu.get_barrier_semaphore()
    greeted = (
        [dev(zh=(z + d) % 8 // 4, zl=(z + d) % 4) for d in range(1, 8)]
        + [dev(x=near_x(dx), y=near_y(dy)) for dx, dy in PLANE]
        + [sibling]
    )
    for device in greeted:
        pl.semaphore_signal(barrier, inc=1, device_id=device, device_id_type=MESH)

    obs[n_words * 8 :, :] = jnp.zeros((obs.shape[0] - n_words * 8, 128), jnp.int32)
    pull[...] = jnp.zeros_like(pull)
    loads[0].wait()

    def two_masks(k, carry):
        unpack(obs, mask, k, n_words)
        return carry

    lax.fori_loop(0, 4, two_masks, 0)
    loads[1].wait()
    half = pl.ds(pl.multiple_of(h * 64, 64), 64)
    other_half = pl.ds(pl.multiple_of(other * 64, 64), 64)
    spread_f[0, x, y, h] = fac[half, :]

    pl.semaphore_wait(barrier, len(greeted))

    for source, *targets in NEAR:
        @pl.when(zl == source)
        def _():
            for i, target in enumerate(targets):
                start(
                    "z", i, fac.at[half, :], spread_f.at[1, x, y, h],
                    dev(zh=1 - zh, zl=target), track=False,
                )
    for dx, dy in PLANE:
        start(
            "a", SLOT(dx, dy), fac.at[half, :], spread_f.at[0, x, y, h],
            dev(x=near_x(dx), y=near_y(dy)),
        )

    loads[2].wait()
    for k in range(cores.shape[0]):
        rows = slice(128 * k, 128 * k + 128)
        value = jnp.dot(fac[...], cores[k], preferred_element_type=F32)
        left[rows, :] = value.astype(BF16)
        left_t[:, rows] = value.T.astype(BF16)

    for source, *targets in NEAR:
        for i, target in enumerate(targets):
            @pl.when(zl == target)
            def _():
                arrive("z", i, spread_f.at[1, x, y, h])
    for dx, dy in PLANE:
        start(
            "b", SLOT(dx, dy), spread_f.at[1, x, y, h], spread_f.at[1, x, y, h],
            dev(x=near_x(dx), y=near_y(dy)),
        )

    def forward(kind, part_of):
        for u, dx in enumerate(ORDER):
            for dy in range(4):
                if dx or dy:
                    slot = SLOT((4 - dx) % 4, (4 - dy) % 4)
                    arrive(kind, slot, spread_f.at[part_of, near_x(dx), near_y(dy), h])
            group = spread_f.at[part_of, near_x(dx), :, h]
            start("fwd", part_of * 4 + u, group, group, sibling, track=part_of == 0)

    forward("a", 0)
    loads[3].wait()

    def place(t):
        part_of, u = t // 4, t % 4
        dx = u + (u // 2) * (5 - 2 * u)
        return part_of, dx, (x + dx) % 4

    def settle(t):
        part_of, dx, group = place(t)
        arrive("swap", t, swapped.at[t])
        terms = blk[t, half, :] + swapped[t]
        for j in range(4):
            r1_out[t, j] = terms[:, 128 * j : 128 * j + 128].astype(ROWS_TYPE)

        @pl.when(dx == 0)
        def _():
            lanes = pl.ds(pl.multiple_of(y * 128, 128), 128)
            acc[part_of] = blk[t, half, lanes] + swapped[t, :, lanes]

        def hand(dy):
            slot = part_of * 15 + dx * 4 + dy - 1
            start(
                "r1", slot, r1_out.at[t, near_y(dy)], r1_in.at[slot],
                dev(x=group, y=near_y(dy)), track=False,
            )

        for dy in (2, 1, 3):
            hand(dy)

        @pl.when(dx != 0)
        def _():
            hand(0)

    def step(t, carry):
        part_of, dx, group = place(t)

        @pl.when(t == 3)
        def _():
            forward("b", 1)

        arrive("fwd", t, spread_f.at[part_of, group, :, other])
        rows = spread_f[part_of, group].reshape(512, 128)
        columns = pl.ds(
            pl.multiple_of(group * 1024 + (zh + part_of * (1 - 2 * zh)) * 512, 512), 512
        )
        model = lax.dot_general(left[...], rows, NT, preferred_element_type=F32)
        for k in range(cores.shape[0]):
            here = slice(128 * k, 128 * k + 128)
            diff = model[here] - facts[k, :, columns].astype(F32)
            err[here, :] = diff.astype(BF16) * mask[k, :, columns]
        pull[...] += jnp.dot(err[...], rows, preferred_element_type=F32)
        blk[t] = jnp.dot(left_t[...], err[...], preferred_element_type=F32)
        start("swap", t, blk.at[t, other_half, :], swapped.at[t], sibling, track=False)

        @pl.when(t >= 1)
        def _():
            settle(t - 1)

        return carry

    lax.fori_loop(0, 8, step, 0)

    fac_t = fac[...].astype(F32).T.astype(BF16)
    pull_hi[...] = pull[...].astype(BF16)
    for k in range(cores.shape[0]):
        rows = slice(128 * k, 128 * k + 128)
        value = jnp.dot(fac_t, pull_hi[rows, :], preferred_element_type=F32)
        part[2 * k : 2 * k + 2] = value.reshape(2, 64, 128)
    k1_out[...] = part[...].astype(CORE_TYPE)
    chunk = x * 4 + y
    for dx, dy in PLANE:
        start(
            "k1", SLOT(dx, dy), k1_out.at[near_x(dx) * 4 + near_y(dy)],
            k1_in.at[SLOT(dx, dy)], dev(x=near_x(dx), y=near_y(dy)),
        )
    own_value = jnp.zeros((128, 128), F32)
    for k in range(cores.shape[0]):
        rows = slice(128 * k, 128 * k + 128)
        high = pull_hi[rows, :]
        low = (pull[rows, :] - high.astype(F32)).astype(BF16)
        own_value += lax.dot_general(cores[k], high, NT, preferred_element_type=F32)
        own_value += lax.dot_general(cores[k], low, NT, preferred_element_type=F32)
    own[...] = own_value
    start("own", 0, own.at[other_half, :], own_in, sibling)
    settle(7)

    value = part[chunk]
    for i in range(15):
        arrive("k1", i, k1_in.at[i])
        value = value + k1_in[i].astype(F32)
    k_small[0] = value
    start("k3", 0, k_small.at[0], k3_in, dev(zh=1 - zh))

    arrive("own", 0, own_in)
    sums = [acc[0] + own[half, :] + own_in[...], acc[1]]
    for i in range(30):
        arrive("r1", i, r1_in.at[i])
        sums[i // 15] = sums[i // 15] + r1_in[i].astype(F32)
    ring[z] = sums[0]
    total[0] = sums[1]
    for d in range(4):
        start("zr", d + 3, total.at[0], ring.at[z], dev(zh=1 - zh, zl=(zl + d) % 4))
    for d in (1, 2, 3):
        start("zr", d - 1, ring.at[z], ring.at[z], dev(zl=(zl + d) % 4))

    n_all = facts.shape[2]
    n_rel = cores.shape[0] * lax.axis_size("rel")
    arrive("k3", 0, k3_in)
    k_final[chunk] = (k_small[0] + k3_in[...]) * (fac.shape[1] / n_all)
    for dx, dy in PLANE:
        start(
            "k5", SLOT(dx, dy), k_final.at[chunk], k_final.at[chunk],
            dev(x=near_x(dx), y=near_y(dy)),
        )

    for d in (1, 2, 3):
        arrive("zr", d - 1, ring.at[zh * 4 + (zl - d + 4) % 4])
    for d in range(4):
        arrive("zr", d + 3, ring.at[(1 - zh) * 4 + (zl - d + 4) % 4])
    summed = ring[0]
    for i in range(1, 8):
        summed = summed + ring[i]
    total[1] = summed * (1.0 / math.sqrt(n_all * n_rel))
    start("fin", 0, total.at[1], total_in.at[h], sibling)
    total_in[h] = total[1]

    for dx, dy in PLANE:
        slot = SLOT((4 - dx) % 4, (4 - dy) % 4)
        arrive("k5", slot, k_final.at[near_x(dx) * 4 + near_y(dy)])
    store = pltpu.make_async_copy(k_final, gc_hbm, local.at[0])
    store.start()
    arrive("fin", 0, total_in.at[other])
    gf_ref[...] = total_in[...].reshape(gf_ref.shape).T

    for kind, index, src in pending:
        sent(kind, index, src)
    for source, *targets in NEAR:
        @pl.when(zl == source)
        def _():
            for i in range(len(targets)):
                sent("z", i, fac.at[half, :])
    for t in range(8):
        sent("swap", t, swapped.at[t])
    for i in range(4):
        sent("fwd", 4 + i, spread_f.at[1, 0, :, h])
    for i in range(30):
        sent("r1", i, r1_in.at[i])
    store.wait()


def deliver_kernel(gf_in, gc_in, gf_out, gc_out, gf, gc, sems):
    count = gc_in.shape[0] // 4
    pieces = [(gf_in, gf, gf_out)]
    for first in range(0, gc_in.shape[0], count):
        at = pl.ds(first, count)
        pieces.append((gc_in.at[at], gc.at[at], gc_out.at[at]))
    loads = [pltpu.make_async_copy(p[0], p[1], sems.at[0, i]) for i, p in enumerate(pieces)]
    stores = [pltpu.make_async_copy(p[1], p[2], sems.at[1, i]) for i, p in enumerate(pieces)]
    for load in loads:
        load.start()
    for load, store in zip(loads, stores):
        load.wait()
        store.start()
    for store in stores:
        store.wait()


def per_device(facts, observed, factors, cores):
    n_rel, n_own, n_all = facts.shape
    rank = factors.shape[1]
    vmem = pltpu.VMEM
    anywhere = pl.BlockSpec(memory_space=pl.ANY)
    inside = pl.BlockSpec(memory_space=pltpu.VMEM)
    n_words = observed.shape[2]
    words = jnp.transpose(observed, (2, 0, 1)).reshape(n_words * n_rel, n_own)
    half = rank // 2
    shapes = (
        jax.ShapeDtypeStruct((n_own, rank), F32),
        jax.ShapeDtypeStruct((2 * n_rel, half, rank), F32),
    )
    rows, cores_grad = pl.pallas_call(
        kernel,
        out_shape=shapes,
        in_specs=[anywhere] * 4,
        out_specs=(inside, anywhere),
        scratch_shapes=[
            vmem(facts.shape, BF16),
            vmem((pl.cdiv(n_words, 128) * 128 * n_rel, n_own), jnp.int32),
            vmem(factors.shape, BF16),
            vmem(cores.shape, BF16),
            vmem(facts.shape, BF16),
            vmem((n_rel * n_own, rank), BF16),
            vmem((rank, n_rel * n_own), BF16),
            vmem((n_rel * n_own, 512), BF16),
            vmem((n_rel * n_own, rank), F32),
            vmem((n_rel * n_own, rank), BF16),
            vmem((2, 4, 4, 2, half, rank), BF16),
            vmem((8, rank, 512), F32),
            vmem((8, half, 512), F32),
            vmem((2, half, 128), F32),
            vmem((8, 4, half, 128), ROWS_TYPE),
            vmem((30, half, 128), ROWS_TYPE),
            vmem((8, half, 128), F32),
            vmem((rank, n_own), F32),
            vmem((half, 128), F32),
            vmem((2, half, 128), F32),
            vmem((2, half, 128), F32),
            vmem((2 * n_rel, half, rank), F32),
            vmem((2 * n_rel, half, rank), CORE_TYPE),
            vmem((15, half, rank), CORE_TYPE),
            vmem((1, half, rank), F32),
            vmem((half, rank), F32),
            vmem((2 * n_rel, half, rank), F32),
            pltpu.SemaphoreType.DMA((4,)),
            pltpu.SemaphoreType.DMA((TOTAL,)),
            pltpu.SemaphoreType.DMA((TOTAL,)),
        ],
        compiler_params=pltpu.CompilerParams(
            collective_id=0, has_side_effects=True, vmem_limit_bytes=56 * 2**20
        ),
        cost_estimate=pl.CostEstimate(
            flops=6 * n_rel * n_own * n_all * rank,
            bytes_accessed=facts.size * 2 + observed.size * 4,
            transcendentals=0,
        ),
        name="rescal_gradients",
    )(facts, words, factors, cores)
    rows, cores_grad = pl.pallas_call(
        deliver_kernel,
        out_shape=shapes,
        in_specs=[anywhere] * 2,
        out_specs=(anywhere, anywhere),
        scratch_shapes=[
            vmem(shapes[0].shape, F32),
            vmem(shapes[1].shape, F32),
            pltpu.SemaphoreType.DMA((2, 5)),
        ],
        name="deliver",
    )(rows, cores_grad)
    return rows, cores_grad.reshape(n_rel, rank, rank)


def solution(mesh):
    return jax.shard_map(
        per_device,
        mesh=mesh,
        in_specs=(
            P("rel", "ent", None),
            P("rel", "ent", None),
            P("ent", None),
            P("rel", None, None),
        ),
        out_specs=(P("ent", None), P("rel", None, None)),
        check_vma=False,
    )
```

time: 911 us -> 54.9 us (0.06)
  the two profiles are of different devices: /device:TPU:1 before, /device:TPU:24 now
where the time goes in v2:
time: 54.9 us; the launch traced here: 54.8 us
  Pallas kernels  54.2 us (99%)
  between operations  0.64 us (1%)
    pallas_call x1, Pallas kernels, per_device(): pl.pallas_call(kernel, out_shape=shapes, in_specs=[anywhere] * 4, out_spe...  52.3 us
    pallas_call x1, Pallas kernels, per_device(): pl.pallas_call(deliver_kernel, out_shape=shapes, in_specs=[anywhere] * 2,...  1.87 us

profile of v2, /device:TPU:24, one launch (start us, length us, event | category | flops | bytes accessed | tf_op | source)
XLA Modules:
  0.0 54.8 jit_solution(17661260183792418986)
XLA Ops:
  0.6 52.3 %rescal_gradients.1 = (f32[128,128]{1,0:T(8,128)}, f32[16,64,128]{2,1,0:T(8,128)}) custom-call(bf16[8,128,4096]{2,1,0:T(8,128)(2,1)} %facts_hbm.1, s32[2528,128]{1,0:T(8,128)} %bitcast.4, bf16[128,128]{1,0:T(8,128)(2,1)} %fac_hbm.1, bf16[8,128,128]{2,1,0:T(8,128)(2,1)} %cores_hbm.1), custom_call_target="tpu_custom_call" | custom-call | flops 3221225472 | bytes 9682944 | tf_op jit(solution)/shard_map/rescal_gradients/pallas_call | solution.py:349
  52.9 1.9 %deliver.1 = (f32[128,128]{1,0:T(8,128)}, f32[16,64,128]{2,1,0:T(8,128)}) custom-call(f32[128,128]{1,0:T(8,128)} %get-tuple-element.6.gf_in, f32[16,64,128]{2,1,0:T(8,128)} %get-tuple-element.7.gc_in), custom_call_target="tpu_custom_call" | custom-call | tf_op jit(solution)/shard_map/deliver/pallas_call | solution.py:396

commit v3 on v2

--- a/solution.py
+++ b/solution.py
@@ -12,6 +12,7 @@
 NT = (((1,), (1,)), ((), ()))
 ROWS_TYPE = BF16
 CORE_TYPE = F32
+EARLY = 4
 
 COUNTS = dict(a=15, b=15, z=2, fwd=8, swap=8, r1=30, zr=7, own=1, fin=1, k1=15, k3=1, k5=15)
 BASE, TOTAL = {}, 0
@@ -28,7 +29,7 @@
 NEAR = ((0, 3, 2), (3, 0, 1))
 
 
-def unpack(obs, mask, k, n_words):
+def unpack(obs, mask, k):
     rows = obs.shape[0] // 8
     low_half = obs[pl.ds(k, rows, stride=8), :]
     high_half = obs[pl.ds(k + 4, rows, stride=8), :]
@@ -52,10 +53,10 @@
 
 
 def kernel(
-    facts_hbm, obs_hbm, fac_hbm, cores_hbm, gf_ref, gc_hbm,
-    facts, obs, fac, cores, mask, left, left_t, err, pull, pull_hi, spread_f,
+    facts_hbm, obs_hbm, fac_hbm, cores_hbm, gf_hbm, gc_hbm,
+    facts, obs, fac, cores, mask, left, left_t, err, pull, spread_f,
     blk, swapped, acc, r1_out, r1_in, ring, own, own_in, total, total_in,
-    part, k1_out, k1_in, k_small, k3_in, k_final,
+    part, k1_out, k1_in, k_small, k3_in, k_final, result,
     local, send, recv,
 ):
     rel, ent = lax.axis_index("rel"), lax.axis_index("ent")
@@ -91,14 +92,6 @@
     def sent(kind, index, src):
         message(kind, index, src, src, sibling).wait_send()
 
-    loads = [
-        pltpu.make_async_copy(obs_hbm, obs.at[pl.ds(0, n_words * 8), :], local.at[1]),
-        pltpu.make_async_copy(fac_hbm, fac, local.at[0]),
-        pltpu.make_async_copy(cores_hbm, cores, local.at[2]),
-        pltpu.make_async_copy(facts_hbm, facts, local.at[3]),
-    ]
-    for load in loads:
-        load.start()
     barrier = pltpu.get_barrier_semaphore()
     greeted = (
         [dev(zh=(z + d) % 8 // 4, zl=(z + d) % 4) for d in range(1, 8)]
@@ -107,21 +100,21 @@
     )
     for device in greeted:
         pl.semaphore_signal(barrier, inc=1, device_id=device, device_id_type=MESH)
+    loads = [
+        pltpu.make_async_copy(obs_hbm, obs.at[pl.ds(0, n_words * 8), :], local.at[1]),
+        pltpu.make_async_copy(fac_hbm, fac, local.at[0]),
+        pltpu.make_async_copy(cores_hbm, cores, local.at[2]),
+        pltpu.make_async_copy(facts_hbm, facts, local.at[3]),
+    ]
+    for i in (1, 0, 2, 3):
+        loads[i].start()
 
     obs[n_words * 8 :, :] = jnp.zeros((obs.shape[0] - n_words * 8, 128), jnp.int32)
     pull[...] = jnp.zeros_like(pull)
-    loads[0].wait()
-
-    def two_masks(k, carry):
-        unpack(obs, mask, k, n_words)
-        return carry
-
-    lax.fori_loop(0, 4, two_masks, 0)
     loads[1].wait()
     half = pl.ds(pl.multiple_of(h * 64, 64), 64)
     other_half = pl.ds(pl.multiple_of(other * 64, 64), 64)
     spread_f[0, x, y, h] = fac[half, :]
-
     pl.semaphore_wait(barrier, len(greeted))
 
     for source, *targets in NEAR:
@@ -138,13 +131,13 @@
             dev(x=near_x(dx), y=near_y(dy)),
         )
 
-    loads[2].wait()
-    for k in range(cores.shape[0]):
-        rows = slice(128 * k, 128 * k + 128)
-        value = jnp.dot(fac[...], cores[k], preferred_element_type=F32)
-        left[rows, :] = value.astype(BF16)
-        left_t[:, rows] = value.T.astype(BF16)
-
+    loads[0].wait()
+
+    def two_masks(k, carry):
+        unpack(obs, mask, k)
+        return carry
+
+    lax.fori_loop(0, EARLY, two_masks, 0)
     for source, *targets in NEAR:
         for i, target in enumerate(targets):
             @pl.when(zl == target)
@@ -156,6 +149,16 @@
             dev(x=near_x(dx), y=near_y(dy)),
         )
 
+    lax.fori_loop(EARLY, 4, two_masks, 0)
+    loads[2].wait()
+    wide = jnp.concatenate([cores[k] for k in range(cores.shape[0])], axis=1)
+    lefts = jnp.dot(fac[...], wide, preferred_element_type=F32)
+    for k in range(cores.shape[0]):
+        rows = slice(128 * k, 128 * k + 128)
+        value = lefts[:, rows]
+        left[rows, :] = value.astype(BF16)
+        left_t[:, rows] = value.T.astype(BF16)
+
     def forward(kind, part_of):
         for u, dx in enumerate(ORDER):
             for dy in range(4):
@@ -199,8 +202,13 @@
         def _():
             hand(0)
 
+    def pass_on(t):
+        blk[t] = jnp.dot(left_t[...], err[t % 4], preferred_element_type=F32)
+        start("swap", t, blk.at[t, other_half, :], swapped.at[t], sibling, track=False)
+
     def step(t, carry):
         part_of, dx, group = place(t)
+        u = t % 4
 
         @pl.when(t == 3)
         def _():
@@ -215,12 +223,14 @@
         for k in range(cores.shape[0]):
             here = slice(128 * k, 128 * k + 128)
             diff = model[here] - facts[k, :, columns].astype(F32)
-            err[here, :] = diff.astype(BF16) * mask[k, :, columns]
-        pull[...] += jnp.dot(err[...], rows, preferred_element_type=F32)
-        blk[t] = jnp.dot(left_t[...], err[...], preferred_element_type=F32)
-        start("swap", t, blk.at[t, other_half, :], swapped.at[t], sibling, track=False)
-
-        @pl.when(t >= 1)
+            err[u, here, :] = diff.astype(BF16) * mask[k, :, columns]
+        pull[...] += jnp.dot(err[u], rows, preferred_element_type=F32)
+
+        @pl.when(t < 4)
+        def _():
+            pass_on(t)
+
+        @pl.when((t >= 1) & (t < 5))
         def _():
             settle(t - 1)
 
@@ -229,27 +239,39 @@
     lax.fori_loop(0, 8, step, 0)
 
     fac_t = fac[...].astype(F32).T.astype(BF16)
-    pull_hi[...] = pull[...].astype(BF16)
+    stack = lambda value: jnp.concatenate(
+        [value[128 * k : 128 * k + 128] for k in range(cores.shape[0])], axis=1
+    )
+    pulls = stack(pull[...])
+    high = pulls.astype(BF16)
+    core_terms = jnp.dot(fac_t, high, preferred_element_type=F32)
     for k in range(cores.shape[0]):
-        rows = slice(128 * k, 128 * k + 128)
-        value = jnp.dot(fac_t, pull_hi[rows, :], preferred_element_type=F32)
-        part[2 * k : 2 * k + 2] = value.reshape(2, 64, 128)
-    k1_out[...] = part[...].astype(CORE_TYPE)
+        value = core_terms[:, 128 * k : 128 * k + 128].reshape(2, 64, 128)
+        part[2 * k : 2 * k + 2] = value
+        k1_out[2 * k : 2 * k + 2] = value.astype(CORE_TYPE)
     chunk = x * 4 + y
     for dx, dy in PLANE:
         start(
             "k1", SLOT(dx, dy), k1_out.at[near_x(dx) * 4 + near_y(dy)],
             k1_in.at[SLOT(dx, dy)], dev(x=near_x(dx), y=near_y(dy)),
         )
-    own_value = jnp.zeros((128, 128), F32)
-    for k in range(cores.shape[0]):
-        rows = slice(128 * k, 128 * k + 128)
-        high = pull_hi[rows, :]
-        low = (pull[rows, :] - high.astype(F32)).astype(BF16)
-        own_value += lax.dot_general(cores[k], high, NT, preferred_element_type=F32)
-        own_value += lax.dot_general(cores[k], low, NT, preferred_element_type=F32)
-    own[...] = own_value
+    low = (pulls - high.astype(F32)).astype(BF16)
+    own[...] = lax.dot_general(
+        jnp.concatenate([wide, wide], axis=1), jnp.concatenate([high, low], axis=1), NT,
+        preferred_element_type=F32,
+    )
     start("own", 0, own.at[other_half, :], own_in, sibling)
+
+    def late(t, carry):
+        pass_on(t)
+
+        @pl.when(t >= 5)
+        def _():
+            settle(t - 1)
+
+        return carry
+
+    lax.fori_loop(4, 8, late, 0)
     settle(7)
 
     value = part[chunk]
@@ -274,12 +296,13 @@
     n_all = facts.shape[2]
     n_rel = cores.shape[0] * lax.axis_size("rel")
     arrive("k3", 0, k3_in)
-    k_final[chunk] = (k_small[0] + k3_in[...]) * (fac.shape[1] / n_all)
+    k_final[...] = (k_small[0] + k3_in[...]) * (fac.shape[1] / n_all)
     for dx, dy in PLANE:
         start(
-            "k5", SLOT(dx, dy), k_final.at[chunk], k_final.at[chunk],
-            dev(x=near_x(dx), y=near_y(dy)),
-        )
+            "k5", SLOT(dx, dy), k_final, gc_hbm.at[chunk], dev(x=near_x(dx), y=near_y(dy)),
+        )
+    store = pltpu.make_async_copy(k_final, gc_hbm.at[chunk], local.at[0])
+    store.start()
 
     for d in (1, 2, 3):
         arrive("zr", d - 1, ring.at[zh * 4 + (zl - d + 4) % 4])
@@ -292,13 +315,14 @@
     start("fin", 0, total.at[1], total_in.at[h], sibling)
     total_in[h] = total[1]
 
+    arrive("fin", 0, total_in.at[other])
+    result[...] = total_in[...].reshape(result.shape).T
+    store_rows = pltpu.make_async_copy(result, gf_hbm, local.at[1])
+    store_rows.start()
+
     for dx, dy in PLANE:
         slot = SLOT((4 - dx) % 4, (4 - dy) % 4)
-        arrive("k5", slot, k_final.at[near_x(dx) * 4 + near_y(dy)])
-    store = pltpu.make_async_copy(k_final, gc_hbm, local.at[0])
-    store.start()
-    arrive("fin", 0, total_in.at[other])
-    gf_ref[...] = total_in[...].reshape(gf_ref.shape).T
+        arrive("k5", slot, gc_hbm.at[near_x(dx) * 4 + near_y(dy)])
 
     for kind, index, src in pending:
         sent(kind, index, src)
@@ -314,23 +338,7 @@
     for i in range(30):
         sent("r1", i, r1_in.at[i])
     store.wait()
-
-
-def deliver_kernel(gf_in, gc_in, gf_out, gc_out, gf, gc, sems):
-    count = gc_in.shape[0] // 4
-    pieces = [(gf_in, gf, gf_out)]
-    for first in range(0, gc_in.shape[0], count):
-        at = pl.ds(first, count)
-        pieces.append((gc_in.at[at], gc.at[at], gc_out.at[at]))
-    loads = [pltpu.make_async_copy(p[0], p[1], sems.at[0, i]) for i, p in enumerate(pieces)]
-    stores = [pltpu.make_async_copy(p[1], p[2], sems.at[1, i]) for i, p in enumerate(pieces)]
-    for load in loads:
-        load.start()
-    for load, store in zip(loads, stores):
-        load.wait()
-        store.start()
-    for store in stores:
-        store.wait()
+    store_rows.wait()
 
 
 def per_device(facts, observed, factors, cores):
@@ -338,7 +346,6 @@
     rank = factors.shape[1]
     vmem = pltpu.VMEM
     anywhere = pl.BlockSpec(memory_space=pl.ANY)
-    inside = pl.BlockSpec(memory_space=pltpu.VMEM)
     n_words = observed.shape[2]
     words = jnp.transpose(observed, (2, 0, 1)).reshape(n_words * n_rel, n_own)
     half = rank // 2
@@ -348,9 +355,9 @@
     )
     rows, cores_grad = pl.pallas_call(
         kernel,
-        out_shape=shapes,
+        out_shape=tuple(vmem(shape.shape, shape.dtype) for shape in shapes),
         in_specs=[anywhere] * 4,
-        out_specs=(inside, anywhere),
+        out_specs=(anywhere, anywhere),
         scratch_shapes=[
             vmem(facts.shape, BF16),
             vmem((pl.cdiv(n_words, 128) * 128 * n_rel, n_own), jnp.int32),
@@ -359,9 +366,8 @@
             vmem(facts.shape, BF16),
             vmem((n_rel * n_own, rank), BF16),
             vmem((rank, n_rel * n_own), BF16),
-            vmem((n_rel * n_own, 512), BF16),
+            vmem((4, n_rel * n_own, 512), BF16),
             vmem((n_rel * n_own, rank), F32),
-            vmem((n_rel * n_own, rank), BF16),
             vmem((2, 4, 4, 2, half, rank), BF16),
             vmem((8, rank, 512), F32),
             vmem((8, half, 512), F32),
@@ -378,7 +384,8 @@
             vmem((15, half, rank), CORE_TYPE),
             vmem((1, half, rank), F32),
             vmem((half, rank), F32),
-            vmem((2 * n_rel, half, rank), F32),
+            vmem((half, rank), F32),
+            vmem((n_own, rank), F32),
             pltpu.SemaphoreType.DMA((4,)),
             pltpu.SemaphoreType.DMA((TOTAL,)),
             pltpu.SemaphoreType.DMA((TOTAL,)),
@@ -393,18 +400,6 @@
         ),
         name="rescal_gradients",
     )(facts, words, factors, cores)
-    rows, cores_grad = pl.pallas_call(
-        deliver_kernel,
-        out_shape=shapes,
-        in_specs=[anywhere] * 2,
-        out_specs=(anywhere, anywhere),
-        scratch_shapes=[
-            vmem(shapes[0].shape, F32),
-            vmem(shapes[1].shape, F32),
-            pltpu.SemaphoreType.DMA((2, 5)),
-        ],
-        name="deliver",
-    )(rows, cores_grad)
     return rows, cores_grad.reshape(n_rel, rank, rank)
 
 

time: 54.9 us -> 50.1 us (0.913)
  the two profiles are of different devices: /device:TPU:24 before, /device:TPU:1 now
where the time goes in v3:
time: 50.1 us
  Pallas kernels  48 us (96%)
  local copies, waits for them, and re-layouts  1.42 us (3%)
  between operations  0.64 us (1%)
    pallas_call x1, Pallas kernels, per_device(): pl.pallas_call(kernel, out_shape=tuple((vmem(shape.shape, shape.dtype) fo...  48 us
    unnamed x2, local copies, waits for them, and re-layouts  1.42 us

profile of v3, /device:TPU:1, one launch (start us, length us, event | category | flops | bytes accessed | tf_op | source)
XLA Modules:
  0.0 50.1 jit_solution(13785608242320086963)
XLA Ops:
  0.6 48.0 %rescal_gradients.1 = (f32[128,128]{1,0:T(8,128)S(1)}, f32[16,64,128]{2,1,0:T(8,128)S(1)}) custom-call(bf16[8,128,4096]{2,1,0:T(8,128)(2,1)} %facts_hbm.1, s32[2528,128]{1,0:T(8,128)} %bitcast.5, bf16[128,128]{1,0:T(8,128)(2,1)} %fac_hbm.1, bf16[8,128,128]{2,1,0:T(8,128)(2,1)} %cores_hbm.1), custom_call_target="tpu_custom_call" | custom-call | flops 3221225472 | bytes 9682944 | tf_op jit(solution)/shard_map/rescal_gradients/pallas_call | solution.py:356
  48.6 0.6 %copy.8 = f32[128,128]{1,0:T(8,128)} copy(f32[128,128]{1,0:T(8,128)S(1)} %get-tuple-element.6) | data formatting | bytes 131072
  49.3 0.8 %copy.9 = f32[8,128,128]{2,1,0:T(8,128)} copy(f32[8,128,128]{2,1,0:T(8,128)S(1)} %bitcast.4) | data formatting | bytes 1048576

commit v4 on v3

--- a/solution.py
+++ b/solution.py
@@ -11,8 +11,7 @@
 MESH = pl.DeviceIdType.MESH
 NT = (((1,), (1,)), ((), ()))
 ROWS_TYPE = BF16
-CORE_TYPE = F32
-EARLY = 4
+CORE_TYPE = BF16
 
 COUNTS = dict(a=15, b=15, z=2, fwd=8, swap=8, r1=30, zr=7, own=1, fin=1, k1=15, k3=1, k5=15)
 BASE, TOTAL = {}, 0
@@ -92,6 +91,14 @@
     def sent(kind, index, src):
         message(kind, index, src, src, sibling).wait_send()
 
+    loads = [
+        pltpu.make_async_copy(obs_hbm, obs.at[pl.ds(0, n_words * 8), :], local.at[1]),
+        pltpu.make_async_copy(fac_hbm, fac, local.at[0]),
+        pltpu.make_async_copy(cores_hbm, cores, local.at[2]),
+        pltpu.make_async_copy(facts_hbm, facts, local.at[3]),
+    ]
+    loads[1].start()
+    loads[0].start()
     barrier = pltpu.get_barrier_semaphore()
     greeted = (
         [dev(zh=(z + d) % 8 // 4, zl=(z + d) % 4) for d in range(1, 8)]
@@ -100,14 +107,8 @@
     )
     for device in greeted:
         pl.semaphore_signal(barrier, inc=1, device_id=device, device_id_type=MESH)
-    loads = [
-        pltpu.make_async_copy(obs_hbm, obs.at[pl.ds(0, n_words * 8), :], local.at[1]),
-        pltpu.make_async_copy(fac_hbm, fac, local.at[0]),
-        pltpu.make_async_copy(cores_hbm, cores, local.at[2]),
-        pltpu.make_async_copy(facts_hbm, facts, local.at[3]),
-    ]
-    for i in (1, 0, 2, 3):
-        loads[i].start()
+    loads[2].start()
+    loads[3].start()
 
     obs[n_words * 8 :, :] = jnp.zeros((obs.shape[0] - n_words * 8, 128), jnp.int32)
     pull[...] = jnp.zeros_like(pull)
@@ -137,7 +138,17 @@
         unpack(obs, mask, k)
         return carry
 
-    lax.fori_loop(0, EARLY, two_masks, 0)
+    lax.fori_loop(0, 4, two_masks, 0)
+    loads[2].wait()
+    wide = jnp.concatenate([cores[k] for k in range(cores.shape[0])], axis=1)
+    lefts = jnp.dot(fac[...], wide, preferred_element_type=F32)
+    fac_t = fac[...].astype(F32).T.astype(BF16)
+    for k in range(cores.shape[0]):
+        rows = slice(128 * k, 128 * k + 128)
+        value = lefts[:, rows]
+        left[rows, :] = value.astype(BF16)
+        left_t[:, rows] = value.T.astype(BF16)
+
     for source, *targets in NEAR:
         for i, target in enumerate(targets):
             @pl.when(zl == target)
@@ -149,16 +160,6 @@
             dev(x=near_x(dx), y=near_y(dy)),
         )
 
-    lax.fori_loop(EARLY, 4, two_masks, 0)
-    loads[2].wait()
-    wide = jnp.concatenate([cores[k] for k in range(cores.shape[0])], axis=1)
-    lefts = jnp.dot(fac[...], wide, preferred_element_type=F32)
-    for k in range(cores.shape[0]):
-        rows = slice(128 * k, 128 * k + 128)
-        value = lefts[:, rows]
-        left[rows, :] = value.astype(BF16)
-        left_t[:, rows] = value.T.astype(BF16)
-
     def forward(kind, part_of):
         for u, dx in enumerate(ORDER):
             for dy in range(4):
@@ -238,7 +239,6 @@
 
     lax.fori_loop(0, 8, step, 0)
 
-    fac_t = fac[...].astype(F32).T.astype(BF16)
     stack = lambda value: jnp.concatenate(
         [value[128 * k : 128 * k + 128] for k in range(cores.shape[0])], axis=1
     )
@@ -248,13 +248,20 @@
     for k in range(cores.shape[0]):
         value = core_terms[:, 128 * k : 128 * k + 128].reshape(2, 64, 128)
         part[2 * k : 2 * k + 2] = value
-        k1_out[2 * k : 2 * k + 2] = value.astype(CORE_TYPE)
+        if CORE_TYPE != F32:
+            k1_out[2 * k : 2 * k + 2] = value.astype(CORE_TYPE)
+    core_source = part if CORE_TYPE == F32 else k1_out
     chunk = x * 4 + y
     for dx, dy in PLANE:
         start(
-            "k1", SLOT(dx, dy), k1_out.at[near_x(dx) * 4 + near_y(dy)],
+            "k1", SLOT(dx, dy), core_source.at[near_x(dx) * 4 + near_y(dy)],
             k1_in.at[SLOT(dx, dy)], dev(x=near_x(dx), y=near_y(dy)),
         )
+    def late_terms(t, carry):
+        pass_on(t)
+        return carry
+
+    lax.fori_loop(4, 8, late_terms, 0)
     low = (pulls - high.astype(F32)).astype(BF16)
     own[...] = lax.dot_general(
         jnp.concatenate([wide, wide], axis=1), jnp.concatenate([high, low], axis=1), NT,
@@ -262,17 +269,20 @@
     )
     start("own", 0, own.at[other_half, :], own_in, sibling)
 
-    def late(t, carry):
-        pass_on(t)
-
-        @pl.when(t >= 5)
-        def _():
-            settle(t - 1)
-
+    def late_settle(t, carry):
+        settle(t)
         return carry
 
-    lax.fori_loop(4, 8, late, 0)
-    settle(7)
+    lax.fori_loop(4, 8, late_settle, 0)
+
+    arrive("own", 0, own_in)
+    value = acc[0] + own[half, :] + own_in[...]
+    for i in range(15):
+        arrive("r1", i, r1_in.at[i])
+        value = value + r1_in[i].astype(F32)
+    ring[z] = value
+    for d in (1, 2, 3):
+        start("zr", d - 1, ring.at[z], ring.at[z], dev(zl=(zl + d) % 4))
 
     value = part[chunk]
     for i in range(15):
@@ -281,17 +291,13 @@
     k_small[0] = value
     start("k3", 0, k_small.at[0], k3_in, dev(zh=1 - zh))
 
-    arrive("own", 0, own_in)
-    sums = [acc[0] + own[half, :] + own_in[...], acc[1]]
-    for i in range(30):
+    value = acc[1]
+    for i in range(15, 30):
         arrive("r1", i, r1_in.at[i])
-        sums[i // 15] = sums[i // 15] + r1_in[i].astype(F32)
-    ring[z] = sums[0]
-    total[0] = sums[1]
+        value = value + r1_in[i].astype(F32)
+    total[0] = value
     for d in range(4):
         start("zr", d + 3, total.at[0], ring.at[z], dev(zh=1 - zh, zl=(zl + d) % 4))
-    for d in (1, 2, 3):
-        start("zr", d - 1, ring.at[z], ring.at[z], dev(zl=(zl + d) % 4))
 
     n_all = facts.shape[2]
     n_rel = cores.shape[0] * lax.axis_size("rel")
@@ -320,12 +326,9 @@
     store_rows = pltpu.make_async_copy(result, gf_hbm, local.at[1])
     store_rows.start()
 
-    for dx, dy in PLANE:
-        slot = SLOT((4 - dx) % 4, (4 - dy) % 4)
-        arrive("k5", slot, gc_hbm.at[near_x(dx) * 4 + near_y(dy)])
-
     for kind, index, src in pending:
-        sent(kind, index, src)
+        if kind != "k5":
+            sent(kind, index, src)
     for source, *targets in NEAR:
         @pl.when(zl == source)
         def _():
@@ -337,6 +340,14 @@
         sent("fwd", 4 + i, spread_f.at[1, 0, :, h])
     for i in range(30):
         sent("r1", i, r1_in.at[i])
+
+    for dx, dy in PLANE:
+        slot = SLOT((4 - dx) % 4, (4 - dy) % 4)
+        arrive("k5", slot, gc_hbm.at[near_x(dx) * 4 + near_y(dy)])
+
+    for kind, index, src in pending:
+        if kind == "k5":
+            sent(kind, index, src)
     store.wait()
     store_rows.wait()
 

time: 50.1 us -> 47.3 us (0.944)
  Pallas kernels: 48 us -> 45.2 us
    pallas_call x1, Pallas kernels: 48 us -> 45.2 us  [per_device(): pl.pallas_call(kernel, out_shape=tuple((vmem(shape.shape, shape.dtype) fo...]
where the time goes in v4:
time: 47.3 us; the launch traced here: 47.2 us
  Pallas kernels  45.2 us (96%)
  local copies, waits for them, and re-layouts  1.42 us (3%)
  between operations  0.64 us (1%)
    pallas_call x1, Pallas kernels, per_device(): pl.pallas_call(kernel, out_shape=tuple((vmem(shape.shape, shape.dtype) fo...  45.2 us
    unnamed x2, local copies, waits for them, and re-layouts  1.42 us

profile of v4, /device:TPU:1, one launch (start us, length us, event | category | flops | bytes accessed | tf_op | source)
XLA Modules:
  0.0 47.2 jit_solution(15658537812995705448)
XLA Ops:
  0.6 45.2 %rescal_gradients.1 = (f32[128,128]{1,0:T(8,128)S(1)}, f32[16,64,128]{2,1,0:T(8,128)S(1)}) custom-call(bf16[8,128,4096]{2,1,0:T(8,128)(2,1)} %facts_hbm.1, s32[2528,128]{1,0:T(8,128)} %bitcast.5, bf16[128,128]{1,0:T(8,128)(2,1)} %fac_hbm.1, bf16[8,128,128]{2,1,0:T(8,128)(2,1)} %cores_hbm.1), custom_call_target="tpu_custom_call" | custom-call | flops 3221225472 | bytes 9682944 | tf_op jit(solution)/shard_map/rescal_gradients/pallas_call | solution.py:367
  45.8 0.6 %copy.8 = f32[128,128]{1,0:T(8,128)} copy(f32[128,128]{1,0:T(8,128)S(1)} %get-tuple-element.6) | data formatting | bytes 131072
  46.4 0.8 %copy.9 = f32[8,128,128]{2,1,0:T(8,128)} copy(f32[8,128,128]{2,1,0:T(8,128)S(1)} %bitcast.4) | data formatting | bytes 1048576

commit v5 on v4

--- a/solution.py
+++ b/solution.py
@@ -258,7 +258,7 @@
             k1_in.at[SLOT(dx, dy)], dev(x=near_x(dx), y=near_y(dy)),
         )
     def late_terms(t, carry):
-        pass_on(t)
+        pass_on(11 - t)
         return carry
 
     lax.fori_loop(4, 8, late_terms, 0)
@@ -270,7 +270,7 @@
     start("own", 0, own.at[other_half, :], own_in, sibling)
 
     def late_settle(t, carry):
-        settle(t)
+        settle(11 - t)
         return carry
 
     lax.fori_loop(4, 8, late_settle, 0)

time: 47.3 us -> 46.7 us (0.987)
  Pallas kernels: 45.2 us -> 44.5 us
    pallas_call x1, Pallas kernels: 45.2 us -> 44.5 us  [per_device(): pl.pallas_call(kernel, out_shape=tuple((vmem(shape.shape, shape.dtype) fo...]
where the time goes in v5:
time: 46.7 us; the launch traced here: 46.6 us
  Pallas kernels  44.5 us (95%)
  local copies, waits for them, and re-layouts  1.42 us (3%)
  between operations  0.64 us (1%)
    pallas_call x1, Pallas kernels, per_device(): pl.pallas_call(kernel, out_shape=tuple((vmem(shape.shape, shape.dtype) fo...  44.5 us
    unnamed x2, local copies, waits for them, and re-layouts  1.42 us

profile of v5, /device:TPU:1, one launch (start us, length us, event | category | flops | bytes accessed | tf_op | source)
XLA Modules:
  0.0 46.6 jit_solution(15257583717219873125)
XLA Ops:
  0.6 44.5 %rescal_gradients.1 = (f32[128,128]{1,0:T(8,128)S(1)}, f32[16,64,128]{2,1,0:T(8,128)S(1)}) custom-call(bf16[8,128,4096]{2,1,0:T(8,128)(2,1)} %facts_hbm.1, s32[2528,128]{1,0:T(8,128)} %bitcast.5, bf16[128,128]{1,0:T(8,128)(2,1)} %fac_hbm.1, bf16[8,128,128]{2,1,0:T(8,128)(2,1)} %cores_hbm.1), custom_call_target="tpu_custom_call" | custom-call | flops 3221225472 | bytes 9682944 | tf_op jit(solution)/shard_map/rescal_gradients/pallas_call | solution.py:367
  45.2 0.6 %copy.8 = f32[128,128]{1,0:T(8,128)} copy(f32[128,128]{1,0:T(8,128)S(1)} %get-tuple-element.6) | data formatting | bytes 131072
  45.8 0.8 %copy.9 = f32[8,128,128]{2,1,0:T(8,128)} copy(f32[8,128,128]{2,1,0:T(8,128)S(1)} %bitcast.4) | data formatting | bytes 1048576
